TPU v7x, 512 devices: a whole 4x8x8 slice. The times are simulated.
512 devices in a mesh: img: 32 (over y, x_lo, core), seq: 16 (over x_hi, z).
Axes of the slice: x: 4 (x_hi: 2, x_lo: 2; x = x_hi * 2 + x_lo), y: 8, z: 8, core: 2. Of those that a mesh axis runs over, the one named last changes fastest.
Arguments:
- query_rows: bfloat16 [65536, 1536], P(('img', 'seq')), parts along dimension 0, may hold values from -16 to 16
- key_rows: bfloat16 [65536, 1536], P(('img', 'seq')), parts along dimension 0, may hold values from -16 to 16
- value_rows: bfloat16 [65536, 1536], P(('img', 'seq')), parts along dimension 0, may hold values from -6 to 6
- qk_gain: float32 [2, 128], replicated, may hold values from 0.6 to 5.6
- w_latent: bfloat16 [1536, 64], replicated, may hold values from -3 to 3
- conv_in_w: bfloat16 [3, 3, 16, 512], replicated, may hold values from -0.5 to 0.5
- conv_in_b: float32 [512], replicated, may hold values from -3 to 3
- conv_w: bfloat16 [3, 3, 512, 512], P(None, None, None, 'seq'), may hold values from -0.09375 to 0.09375
- conv_b: float32 [512], replicated, may hold values from -3 to 3
Outputs:
- feature_tiles: bfloat16 [512, 16, 32, 512], P(('img', 'seq')), parts along dimension 0
There are 32 independent parts, one for each index of `img`. A program takes and returns all parts, laid end to end along the dimension named above; an argument that names none is the same for every part. Nothing has to cross between parts.
All inputs are finite; a program needn't handle non-finite values.
Results may differ from a plain program's by a relative error of at most 0.017.
The roundings to bfloat16 on the way count: a program that leaves them out, or rounds other values in their place, can miss the bound.
Values may be sent and summed in bfloat16 or wider, within the bound.
No kernel may reach another device: no remote copies, remote signals or barrier semaphores. Data moves between devices by JAX's collectives and lax.ppermute only.
A program may use at most 128 MiB of HBM per device.

v0:
```python
import math

import jax
import jax.numpy as jnp
import numpy as np
from jax import lax
from jax.sharding import PartitionSpec as P

GW = 64


THETA = 10000.0
EPS_NORM = 1e-06
LATENT_SCALE = 0.3611
LATENT_SHIFT = 0.1159


def shifted(block, axis, distance):
    devices = range(lax.axis_size(axis))
    route = [(i - distance, i) for i in devices if i - distance in devices]
    return lax.ppermute(block, axis, route)


def rope_tables(row_ids, col_ids, head_dim):
    t_dims = head_dim // 8
    s_dims = (head_dim - t_dims) // 2
    dim_index = np.arange(head_dim)
    pair_index = dim_index // 2
    t_pairs = t_dims // 2
    s_pairs = s_dims // 2
    axis_id = np.where(pair_index < t_pairs, 0, np.where(pair_index < t_pairs + s_pairs, 1, 2))
    local_index = np.where(
        axis_id == 0,
        pair_index,
        np.where(axis_id == 1, pair_index - t_pairs, pair_index - t_pairs - s_pairs),
    )
    axis_dims = np.where(axis_id == 0, t_dims, s_dims)
    frequency = jnp.asarray((THETA ** (-2.0 * local_index / axis_dims)).astype(np.float32))
    on_rows = jnp.asarray((axis_id == 1).astype(np.float32))
    on_cols = jnp.asarray((axis_id == 2).astype(np.float32))
    angles = (
        row_ids.astype(jnp.float32)[:, None] * on_rows
        + col_ids.astype(jnp.float32)[:, None] * on_cols
    ) * frequency
    return (jnp.cos(angles), jnp.sin(angles))


def pair_turn(head_dim):
    dim_index = np.arange(head_dim)
    turn_table = np.zeros((head_dim, head_dim), np.float32)
    turn_table[dim_index[1::2], dim_index[0::2]] = -1.0
    turn_table[dim_index[0::2], dim_index[1::2]] = 1.0
    return jnp.asarray(turn_table)


def prepare(raw_rows, gain_row, cosine, sine_part, turn_table):
    head_dim = turn_table.shape[0]
    head_count = raw_rows.shape[1] // head_dim
    shaped = raw_rows.astype(jnp.float32).reshape(raw_rows.shape[0], head_count, head_dim)
    mean_sq = jnp.mean(shaped * shaped, axis=2, keepdims=True)
    normed = shaped * lax.rsqrt(mean_sq + EPS_NORM) * gain_row
    turned = jnp.einsum("thd,de->the", normed, turn_table, precision=lax.Precision.HIGHEST)
    return (normed * cosine[:, None, :] + turned * sine_part[:, None, :]).astype(jnp.bfloat16)


def conv_three(padded, weight):
    height = padded.shape[0] - 2
    width_px = padded.shape[1] - 2
    summed = None
    for tap_row in range(3):
        for tap_col in range(3):
            window = padded[tap_row : tap_row + height, tap_col : tap_col + width_px].reshape(
                height * width_px, -1
            )
            contrib = jnp.dot(window, weight[tap_row, tap_col], preferred_element_type=jnp.float32)
            summed = contrib if summed is None else summed + contrib
    return summed.reshape(height, width_px, -1)


def sideways(rim_part, offset):
    return shifted(rim_part, "seq", offset)


def upright(rim_part, offset):
    return shifted(rim_part, "seq", offset)


def extend(field_map, rim_depth, my_col, tile_cols):
    from_left = sideways(field_map[:, -rim_depth:], 1)
    from_right = sideways(field_map[:, :rim_depth], -1)
    from_left = jnp.where(my_col > 0, from_left, jnp.zeros_like(from_left))
    from_right = jnp.where(my_col < tile_cols - 1, from_right, jnp.zeros_like(from_right))
    widened = jnp.concatenate([from_left, field_map, from_right], axis=1)
    from_above = upright(widened[-rim_depth:], tile_cols)
    from_below = upright(widened[:rim_depth], -tile_cols)
    return jnp.concatenate([from_above, widened, from_below], axis=0)


def on_device(
    query_rows, key_rows, value_rows, qk_gain, w_latent, conv_in_w, conv_in_b, conv_w, conv_b
):
    devices = lax.axis_size("seq")
    my_index = lax.axis_index("seq")
    tok_dev = query_rows.shape[0]
    head_dim = qk_gain.shape[1]
    head_count = query_rows.shape[1] // head_dim
    band_rows = tok_dev // GW
    tile_rows = math.isqrt(devices)
    tile_cols = devices // tile_rows
    tile_height = band_rows * tile_cols
    tile_width = GW // tile_cols
    packed = w_latent.shape[1]
    latent_ch = packed // 4
    token_ids = my_index * tok_dev + jnp.arange(tok_dev, dtype=jnp.int32)
    cosine, sine_part = rope_tables(token_ids // GW, token_ids % GW, head_dim)
    turn_table = pair_turn(head_dim)
    queries = prepare(query_rows, qk_gain[0], cosine, sine_part, turn_table)
    keys_ready = prepare(key_rows, qk_gain[1], cosine, sine_part, turn_table)
    values = value_rows.reshape(tok_dev, head_count, head_dim)
    score_scale = 1.0 / math.sqrt(head_dim)
    start_state = (
        jnp.full((head_count, tok_dev), -jnp.inf, jnp.float32),
        jnp.zeros((head_count, tok_dev), jnp.float32),
        jnp.zeros((head_count, tok_dev, head_dim), jnp.float32),
    )
    running = start_state
    keys_piece = lax.all_gather(keys_ready, "seq", axis=0, tiled=True)
    values_piece = lax.all_gather(values, "seq", axis=0, tiled=True)
    piece_rows = keys_piece.shape[0]
    block_rows = math.gcd(piece_rows, 1024)
    keys_blocks = keys_piece.reshape(piece_rows // block_rows, block_rows, head_count, head_dim)
    values_blocks = values_piece.reshape(piece_rows // block_rows, block_rows, head_count, head_dim)

    def one_block(current, blocks):
        best_score, total_mass, weighted = current
        keys_block, values_block = blocks
        scores = (
            jnp.einsum("qhd,khd->hqk", queries, keys_block, preferred_element_type=jnp.float32)
            * score_scale
        )
        newest = jnp.maximum(best_score, jnp.max(scores, axis=2))
        weights = jnp.exp(scores - newest[:, :, None])
        factor = jnp.exp(best_score - newest)
        total_mass = total_mass * factor + jnp.sum(weights, axis=2)
        weighted = weighted * factor[:, :, None] + jnp.einsum(
            "hqk,khd->hqd",
            weights.astype(jnp.bfloat16),
            values_block,
            preferred_element_type=jnp.float32,
        )
        return ((newest, total_mass, weighted), None)

    running, unused = lax.scan(one_block, running, (keys_blocks, values_blocks))
    best_score, total_mass, weighted = running
    attended = (
        (weighted / total_mass[:, :, None])
        .astype(jnp.bfloat16)
        .transpose(1, 0, 2)
        .reshape(tok_dev, head_count * head_dim)
    )
    latent = jnp.dot(attended, w_latent, preferred_element_type=jnp.float32).astype(jnp.bfloat16)
    my_col = my_index % tile_cols
    pieces = latent.reshape(band_rows, tile_cols, tile_width * packed).transpose(1, 0, 2)
    slot_data = jnp.zeros_like(pieces)
    for offset in range(1 - tile_cols, tile_cols):
        target = my_col + offset
        chosen = lax.dynamic_index_in_dim(
            pieces, jnp.clip(target, 0, tile_cols - 1), 0, keepdims=False
        )
        chosen = jnp.where((target >= 0) & (target < tile_cols), chosen, jnp.zeros_like(chosen))
        arrived = chosen if offset == 0 else shifted(chosen, "seq", offset)
        source = my_col - offset
        source_mask = jnp.arange(tile_cols) == source
        slot_data = slot_data + jnp.where(
            source_mask[:, None, None], arrived[None], jnp.zeros_like(slot_data)
        )
    unpacked = slot_data.reshape(tile_height, tile_width, latent_ch, 2, 2).transpose(0, 3, 1, 4, 2)
    unpacked = unpacked.reshape(2 * tile_height, 2 * tile_width, latent_ch)
    latent_z = (unpacked.astype(jnp.float32) / LATENT_SCALE + LATENT_SHIFT).astype(jnp.bfloat16)
    padded_z = extend(latent_z, 1, my_col, tile_cols)
    hidden = jax.nn.silu(conv_three(padded_z, conv_in_w) + conv_in_b).astype(jnp.bfloat16)
    padded_hidden = extend(hidden, 1, my_col, tile_cols)
    result = (
        conv_three(padded_hidden, lax.all_gather(conv_w, "seq", axis=3, tiled=True)) + conv_b
    ).astype(jnp.bfloat16)
    return result[None]


def solution(mesh):
    placed = (
        P(("img", "seq"), None),
        P(("img", "seq"), None),
        P(("img", "seq"), None),
        P(),
        P(),
        P(),
        P(),
        P(None, None, None, "seq"),
        P(),
    )
    return jax.shard_map(
        on_device,
        mesh=mesh,
        in_specs=placed,
        out_specs=P(("img", "seq"), None, None, None),
        check_vma=False,
    )
```

profile of v0, /device:TPU:6, one launch (start us, length us, event | category | flops | bytes accessed | tf_op | source)
XLA Modules:
  0.0 424.9 jit_solution(3760676008562533782)
XLA Ops:
  6.5 2.0 copy.65
  8.6 1.2 copy.61
  10.2 0.8 slice_bitcast_fusion.18
  10.9 1.0 fusion.44
  11.9 2.5 fusion.24
  14.5 0.7 all-gather.8.cloned.1.call-update
  15.9 0.9 fusion.23
  16.8 128.6 %all-gather.6.cloned.1.call-done = bf16[2048,12,128]{0,2,1:T(8,128)(2,1)} async-done(((bf16[128,12,128]{0,2,1:T(8,128)(2,1)}), bf16[2048,12,128]{0,2,1:T(8,128)(2,1)}) %all-gather.6.cloned.1.call-update) | async-done | bytes 6291472 | tf_op jit(solution)/shard_map/all_gather | solution.py:128
  145.4 8.7 %copy.66 = bf16[2048,12,128]{2,0,1:T(8,128)(2,1)} copy(bf16[2048,12,128]{0,2,1:T(8,128)(2,1)} %all-gather.6.cloned.1.call-done) | data formatting | bytes 12582912 | tf_op jit(solution)/shard_map/all_gather | solution.py:128
  154.0 112.8 %all-gather.4.cloned.1.call-done = bf16[2048,12,128]{2,0,1:T(8,128)(2,1)} async-done(((bf16[128,12,128]{2,0,1:T(8,128)(2,1)}), bf16[2048,12,128]{2,0,1:T(8,128)(2,1)}) %all-gather.4.cloned.1.call-update) | async-done | bytes 6291472 | tf_op jit(solution)/shard_map/all_gather | solution.py:127
  266.8 27.7 %while.15 = (s32[]{:T(128)}, f32[12,128]{1,0:T(8,128)S(1)}, f32[12,128]{1,0:T(8,128)S(1)}, f32[12,128,128]{2,1,0:T(8,128)S(1)}, bf16[2,1024,12,128]{3,1,0,2:T(8,...) while((s32[]{:T(128)}, f32[12,128]{1,0:T(8,128)S(1)}, ...), condition=%wide.region_5.6_spmd.clone, body=%wide.region_2.5_spmd.clone.sunk | while | flops 818486784 | bytes 52396180 | solution.py:153
  266.8 5.5 %bitcast_reduce_fusion.2 = (f32[12,128]{1,0:T(8,128)S(1)}, f32[12,1024,128]{2,1,0:T(8,128)}) fusion(bf16[128,12,128]{2,0,1:T(8,128)(2,1)S(1)} %get-tuple-element.237, bf16[2,1024,12,128]{3,1,0,2:T(8,128)(2,1)} %get-tuple-element.236, s32[]{:T(128)S(6)} %copy.116), kind=kOutput, calls=%fused_computation.1.clone.1 | convolution fusion | flops 405797376 | bytes 9836548 | tf_op jit(solution)/shard_map/while/body/eval_jaxpr/qhd,khd->hqk/dot_general | solution.py:138
  272.3 4.0 fusion.104
  276.3 0.6 copy-done.1
  276.9 3.7 fusion.106
  280.6 5.5 %bitcast_reduce_fusion.2 = (f32[12,128]{1,0:T(8,128)S(1)}, f32[12,1024,128]{2,1,0:T(8,128)}) fusion(bf16[128,12,128]{2,0,1:T(8,128)(2,1)S(1)} %get-tuple-element.237, bf16[2,1024,12,128]{3,1,0,2:T(8,128)(2,1)} %get-tuple-element.236, s32[]{:T(128)S(6)} %copy.116), kind=kOutput, calls=%fused_computation.1.clone.1 | convolution fusion | flops 405797376 | bytes 9836548 | tf_op jit(solution)/shard_map/while/body/eval_jaxpr/qhd,khd->hqk/dot_general | solution.py:138
  286.1 4.0 fusion.104
  290.1 0.6 copy-done.1
  290.7 3.7 fusion.106
  295.4 4.6 %collective-permute-start.5 = (bf16[2,1024]{1,0:T(2,128)(2,1)S(1)}, bf16[2,1024]{1,0:T(2,128)(2,1)S(1)}, u32[]{:S(2)}, u32[]{:S(2)}) collective-permute-start(bf16[2,1024]{1,0:T(2,128)(2,1)S(1)} %bitcast.207), channel_id=1, source_target_pairs={{0,3},{1,4},{2,5},{3,6},{4,7},{5,8},{6,9},{7,10},{8,11},{9,12},{10... | collective-permute-start | bytes 12296 | tf_op jit(solution)/shard_map/ppermute | solution.py:21
  300.0 3.5 collective-permute-start.4
  303.5 2.8 collective-permute-start.3
  306.2 6.7 %collective-permute-start.2 = (bf16[2,1024]{1,0:T(2,128)(2,1)S(1)}, bf16[2,1024]{1,0:T(2,128)(2,1)S(1)}, u32[]{:S(2)}, u32[]{:S(2)}) collective-permute-start(bf16[2,1024]{1,0:T(2,128)(2,1)S(1)} %bitcast.204), channel_id=1, source_target_pairs={{1,0},{2,1},{3,2},{4,3},{5,4},{6,5},{7,6},{8,7},{9,8},{10,9},{11,1... | collective-permute-start | bytes 12296 | tf_op jit(solution)/shard_map/ppermute | solution.py:21
  313.0 3.3 collective-permute-start.1
  316.3 4.5 %collective-permute-start = (bf16[2,1024]{1,0:T(2,128)(2,1)S(1)}, bf16[2,1024]{1,0:T(2,128)(2,1)S(1)}, u32[]{:S(2)}, u32[]{:S(2)}) collective-permute-start(bf16[2,1024]{1,0:T(2,128)(2,1)S(1)} %bitcast.202), channel_id=1, source_target_pairs={{3,0},{4,1},{5,2},{6,3},{7,4},{8,5},{9,6},{10,7},{11,8},{12,9},{13... | collective-permute-start | bytes 12296 | tf_op jit(solution)/shard_map/ppermute | solution.py:21
  321.9 2.2 broadcast_in_dim.180
  324.2 2.2 broadcast_in_dim.195
  326.5 2.2 broadcast_in_dim.190
  328.8 3.3 broadcast_in_dim.185
  332.1 3.2 broadcast_in_dim.175
  335.3 3.2 broadcast_in_dim.170
  338.6 3.2 broadcast_in_dim.165
  341.8 7.1 %fusion.31 = bf16[8,2,16,2,16]{3,1,4,2,0:T(2,128)(2,1)} fusion(bf16[8,16,16,2,2]{4,3,2,1,0:T(2,128)(2,1)S(1)} %broadcast_in_dim.195, pred[8]{0:T(512)(128)(4,1)S(1)} %broadcast_in_dim.192, bf16[8,16,16,2,2]{4,3,2,1,0:T(2,128)(2,1)S(1)} %broadcast_in_dim.190, pred[8]{0:T(512)(128)(4,1)S(1)} %broadcast_in_dim.187, ...), kind=kLoop, calls=%fused_computation.59 | loop fusion | flops 139264 | bytes 131128 | tf_op jit(solution)/shard_map/add | solution.py:179
  348.9 3.3 copy.71
  352.3 1.9 collective-permute-start.7
  354.3 4.1 collective-permute-start.6
  358.7 4.8 %collective-permute-done.6 = bf16[16,1,16]{2,1,0:T(2,128)(2,1)S(1)} collective-permute-done((bf16[16,1,16]{2,1,0:T(2,128)(2,1)S(1)}, bf16[16,1,16]{2,1,0:T(2,128)(2,1)S(1)}, u32[]{:S(2)}, u32[]{:S(2)}) %collective-permute-start.6) | collective-permute-done | bytes 544 | tf_op jit(solution)/shard_map/ppermute | solution.py:21
  363.8 1.9 collective-permute-start.9
  365.7 7.8 %collective-permute-start.8 = (bf16[1,34,16]{1,2,0:T(8,128)(2,1)S(1)}, bf16[1,34,16]{1,2,0:T(8,128)(2,1)S(1)}, u32[]{:S(2)}, u32[]{:S(2)}) collective-permute-start(bf16[1,34,16]{1,2,0:T(8,128)(2,1)S(1)} %get-tuple-element.139), channel_id=1, source_target_pairs={{0,4},{1,5},{2,6},{3,7},{4,8},{5,9},{6,10},{7,11},{8,12},{9,13},{1... | collective-permute-start | bytes 3272 | tf_op jit(solution)/shard_map/ppermute | solution.py:21
  373.9 3.6 collective-permute-done.8
  378.7 0.3 fusion.53
  379.0 0.3 convolution_add_fusion.15
  379.4 0.3 convolution_add_fusion.14
  379.7 0.3 convolution_add_fusion.13
  381.9 1.9 collective-permute-start.11
  383.9 3.9 collective-permute-start.10
  387.9 5.4 %collective-permute-done.10 = bf16[16,1,512]{2,1,0:T(2,128)(2,1)S(1)} collective-permute-done((bf16[16,1,512]{2,1,0:T(2,128)(2,1)S(1)}, bf16[16,1,512]{2,1,0:T(2,128)(2,1)S(1)}, u32[]{:S(2)}, u32[]{:S(2)}) %collective-permute-start.10) | collective-permute-done | bytes 16416 | tf_op jit(solution)/shard_map/ppermute | solution.py:21
  393.4 1.9 collective-permute-start.13
  395.3 7.8 %collective-permute-start.12 = (bf16[1,34,512]{2,1,0:T(8,128)(2,1)S(1)}, bf16[1,34,512]{2,1,0:T(8,128)(2,1)S(1)}, u32[]{:S(2)}, u32[]{:S(2)}) collective-permute-start(bf16[1,34,512]{2,1,0:T(8,128)(2,1)S(1)} %get-tuple-element.131), channel_id=1, source_target_pairs={{0,4},{1,5},{2,6},{3,7},{4,8},{5,9},{6,10},{7,11},{8,12},{9,13},{1... | collective-permute-start | bytes 104456 | tf_op jit(solution)/shard_map/ppermute | solution.py:21
  403.1 0.4 pad_maximum_fusion.1
  403.5 4.0 collective-permute-done.12
  407.5 0.4 pad_maximum_fusion
  408.0 1.3 fusion.68
  409.3 1.1 fusion.67
  410.4 1.8 fusion.36
  412.2 1.7 convolution_add_fusion.7
  414.0 0.5 convolution_add_fusion.6
  414.5 0.5 convolution_add_fusion.5
  415.0 0.5 convolution_add_fusion.4
  415.4 0.5 convolution_add_fusion.3
  416.0 0.5 convolution_add_fusion.2
  416.5 0.5 convolution_add_fusion.1
  416.9 0.5 convolution_add_fusion
  417.4 0.9 add_convert_fusion.1
  (131 shorter events, 7.4 us)
Async XLA Ops:
  6.5 288.3 %copy-start = (bf16[1536,64]{0,1:T(8,128)(2,1)S(1)}, bf16[1536,64]{0,1:T(8,128)(2,1)}, u32[]{:S(2)}) copy-start(bf16[1536,64]{0,1:T(8,128)(2,1)} %param.19) | copy-start | bytes 589828
  6.5 9.4 %copy-start.9 = (f32[128,128,1]{1,0,2:T(8,128)S(1)}, f32[128,128,1]{1,0,2:T(8,128)}, u32[]{:S(2)}) copy-start(f32[128,128,1]{1,0,2:T(8,128)} %constant.139) | copy-start | bytes 196612
  6.5 8.7 %copy-start.5 = (bf16[128,1536]{1,0:T(8,128)(2,1)S(1)}, bf16[128,1536]{1,0:T(8,128)(2,1)}, u32[]{:S(2)}) copy-start(bf16[128,1536]{1,0:T(8,128)(2,1)} %param.15) | copy-start | bytes 1179652
  6.5 138.8 %all-gather.6.cloned.1.call-start = ((), (), s32[]{:S(2)}) async-start(), calls=%async_computation.1 | async-start | bytes 6684672 | tf_op jit(solution)/shard_map/all_gather | solution.py:128
  8.6 258.2 %all-gather.4.cloned.1.call-start = ((), (), s32[]{:S(2)}) async-start(), calls=%async_computation | async-start | bytes 6684672 | tf_op jit(solution)/shard_map/all_gather | solution.py:127
  14.4 396.0 %all-gather.8.cloned.1.call-start = ((), (), s32[]{:S(2)}) async-start(), calls=%async_computation.2 | async-start | bytes 5013504 | tf_op jit(solution)/shard_map/all_gather | solution.py:184
  272.3 4.6 %copy-start.1 = (f32[12,1024,128]{2,1,0:T(8,128)S(1)}, f32[12,1024,128]{2,1,0:T(8,128)}, u32[]{:S(2)}) copy-start(f32[12,1024,128]{2,1,0:T(8,128)} %get-tuple-element.211) | copy-start | bytes 18874372 | tf_op jit(solution)/shard_map/while
  286.1 4.6 %copy-start.1 = (f32[12,1024,128]{2,1,0:T(8,128)S(1)}, f32[12,1024,128]{2,1,0:T(8,128)}, u32[]{:S(2)}) copy-start(f32[12,1024,128]{2,1,0:T(8,128)} %get-tuple-element.211) | copy-start | bytes 18874372 | tf_op jit(solution)/shard_map/while
  295.4 20.9 %collective-permute-start.5 = (bf16[2,1024]{1,0:T(2,128)(2,1)S(1)}, bf16[2,1024]{1,0:T(2,128)(2,1)S(1)}, u32[]{:S(2)}, u32[]{:S(2)}) collective-permute-start(bf16[2,1024]{1,0:T(2,128)(2,1)S(1)} %bitcast.207), channel_id=1, source_target_pairs={{0,3},{1,4},{2,5},{3,6},{4,7},{5,8},{6,9},{7,10},{8,11},{9,12},{10... | collective-permute-start | bytes 12296 | tf_op jit(solution)/shard_map/ppermute | solution.py:21
  300.0 26.5 %collective-permute-start.4 = (bf16[2,1024]{1,0:T(2,128)(2,1)S(1)}, bf16[2,1024]{1,0:T(2,128)(2,1)S(1)}, u32[]{:S(2)}, u32[]{:S(2)}) collective-permute-start(bf16[2,1024]{1,0:T(2,128)(2,1)S(1)} %bitcast.206), channel_id=1, source_target_pairs={{0,2},{1,3},{2,4},{3,5},{4,6},{5,7},{6,8},{7,9},{8,10},{9,11},{10,... | collective-permute-start | bytes 12296 | tf_op jit(solution)/shard_map/ppermute | solution.py:21
  303.5 25.3 %collective-permute-start.3 = (bf16[2,1024]{1,0:T(2,128)(2,1)S(1)}, bf16[2,1024]{1,0:T(2,128)(2,1)S(1)}, u32[]{:S(2)}, u32[]{:S(2)}) collective-permute-start(bf16[2,1024]{1,0:T(2,128)(2,1)S(1)} %bitcast.205), channel_id=1, source_target_pairs={{0,1},{1,2},{2,3},{3,4},{4,5},{5,6},{6,7},{7,8},{8,9},{9,10},{10,1... | collective-permute-start | bytes 12296 | tf_op jit(solution)/shard_map/ppermute | solution.py:21
  306.2 25.8 %collective-permute-start.2 = (bf16[2,1024]{1,0:T(2,128)(2,1)S(1)}, bf16[2,1024]{1,0:T(2,128)(2,1)S(1)}, u32[]{:S(2)}, u32[]{:S(2)}) collective-permute-start(bf16[2,1024]{1,0:T(2,128)(2,1)S(1)} %bitcast.204), channel_id=1, source_target_pairs={{1,0},{2,1},{3,2},{4,3},{5,4},{6,5},{7,6},{8,7},{9,8},{10,9},{11,1... | collective-permute-start | bytes 12296 | tf_op jit(solution)/shard_map/ppermute | solution.py:21
  313.0 22.3 %collective-permute-start.1 = (bf16[2,1024]{1,0:T(2,128)(2,1)S(1)}, bf16[2,1024]{1,0:T(2,128)(2,1)S(1)}, u32[]{:S(2)}, u32[]{:S(2)}) collective-permute-start(bf16[2,1024]{1,0:T(2,128)(2,1)S(1)} %bitcast.203), channel_id=1, source_target_pairs={{2,0},{3,1},{4,2},{5,3},{6,4},{7,5},{8,6},{9,7},{10,8},{11,9},{12,... | collective-permute-start | bytes 12296 | tf_op jit(solution)/shard_map/ppermute | solution.py:21
  316.3 22.3 %collective-permute-start = (bf16[2,1024]{1,0:T(2,128)(2,1)S(1)}, bf16[2,1024]{1,0:T(2,128)(2,1)S(1)}, u32[]{:S(2)}, u32[]{:S(2)}) collective-permute-start(bf16[2,1024]{1,0:T(2,128)(2,1)S(1)} %bitcast.202), channel_id=1, source_target_pairs={{3,0},{4,1},{5,2},{6,3},{7,4},{8,5},{9,6},{10,7},{11,8},{12,9},{13... | collective-permute-start | bytes 12296 | tf_op jit(solution)/shard_map/ppermute | solution.py:21
  341.8 36.9 %copy-start.6 = (bf16[3,3,16,512]{3,2,1,0:T(8,128)(2,1)S(1)}, bf16[3,3,16,512]{3,2,1,0:T(8,128)(2,1)}, u32[]{:S(2)}) copy-start(bf16[3,3,16,512]{3,2,1,0:T(8,128)(2,1)} %param.20) | copy-start | bytes 442372
  352.3 6.2 %collective-permute-start.7 = (bf16[16,1,16]{2,1,0:T(2,128)(2,1)S(1)}, bf16[16,1,16]{2,1,0:T(2,128)(2,1)S(1)}, u32[]{:S(2)}, u32[]{:S(2)}) collective-permute-start(bf16[16,1,16]{2,1,0:T(2,128)(2,1)S(1)} %get-tuple-element.141), channel_id=1, source_target_pairs={{1,0},{2,1},{3,2},{4,3},{5,4},{6,5},{7,6},{8,7},{9,8},{10,9},{11,1... | collective-permute-start | bytes 1544 | tf_op jit(solution)/shard_map/ppermute | solution.py:21
  354.3 9.2 %collective-permute-start.6 = (bf16[16,1,16]{2,1,0:T(2,128)(2,1)S(1)}, bf16[16,1,16]{2,1,0:T(2,128)(2,1)S(1)}, u32[]{:S(2)}, u32[]{:S(2)}) collective-permute-start(bf16[16,1,16]{2,1,0:T(2,128)(2,1)S(1)} %get-tuple-element.140), channel_id=1, source_target_pairs={{0,1},{1,2},{2,3},{3,4},{4,5},{5,6},{6,7},{7,8},{8,9},{9,10},{10,1... | collective-permute-start | bytes 1544 | tf_op jit(solution)/shard_map/ppermute | solution.py:21
  363.8 10.2 %collective-permute-start.9 = (bf16[1,34,16]{1,2,0:T(8,128)(2,1)S(1)}, bf16[1,34,16]{1,2,0:T(8,128)(2,1)S(1)}, u32[]{:S(2)}, u32[]{:S(2)}) collective-permute-start(bf16[1,34,16]{1,2,0:T(8,128)(2,1)S(1)} %get-tuple-element.138), channel_id=1, source_target_pairs={{4,0},{5,1},{6,2},{7,3},{8,4},{9,5},{10,6},{11,7},{12,8},{13,9},{1... | collective-permute-start | bytes 3272 | tf_op jit(solution)/shard_map/ppermute | solution.py:21
  365.7 11.8 %collective-permute-start.8 = (bf16[1,34,16]{1,2,0:T(8,128)(2,1)S(1)}, bf16[1,34,16]{1,2,0:T(8,128)(2,1)S(1)}, u32[]{:S(2)}, u32[]{:S(2)}) collective-permute-start(bf16[1,34,16]{1,2,0:T(8,128)(2,1)S(1)} %get-tuple-element.139), channel_id=1, source_target_pairs={{0,4},{1,5},{2,6},{3,7},{4,8},{5,9},{6,10},{7,11},{8,12},{9,13},{1... | collective-permute-start | bytes 3272 | tf_op jit(solution)/shard_map/ppermute | solution.py:21
  380.3 1.3 copy-start.7
  381.9 5.9 %collective-permute-start.11 = (bf16[16,1,512]{2,1,0:T(2,128)(2,1)S(1)}, bf16[16,1,512]{2,1,0:T(2,128)(2,1)S(1)}, u32[]{:S(2)}, u32[]{:S(2)}) collective-permute-start(bf16[16,1,512]{2,1,0:T(2,128)(2,1)S(1)} %get-tuple-element.135), channel_id=1, source_target_pairs={{1,0},{2,1},{3,2},{4,3},{5,4},{6,5},{7,6},{8,7},{9,8},{10,9},{11,1... | collective-permute-start | bytes 49160 | tf_op jit(solution)/shard_map/ppermute | solution.py:21
  383.9 9.4 %collective-permute-start.10 = (bf16[16,1,512]{2,1,0:T(2,128)(2,1)S(1)}, bf16[16,1,512]{2,1,0:T(2,128)(2,1)S(1)}, u32[]{:S(2)}, u32[]{:S(2)}) collective-permute-start(bf16[16,1,512]{2,1,0:T(2,128)(2,1)S(1)} %get-tuple-element.134), channel_id=1, source_target_pairs={{0,1},{1,2},{2,3},{3,4},{4,5},{5,6},{6,7},{7,8},{8,9},{9,10},{10,1... | collective-permute-start | bytes 49160 | tf_op jit(solution)/shard_map/ppermute | solution.py:21
  393.4 10.1 %collective-permute-start.13 = (bf16[1,34,512]{2,1,0:T(8,128)(2,1)S(1)}, bf16[1,34,512]{2,1,0:T(8,128)(2,1)S(1)}, u32[]{:S(2)}, u32[]{:S(2)}) collective-permute-start(bf16[1,34,512]{2,1,0:T(8,128)(2,1)S(1)} %get-tuple-element.130), channel_id=1, source_target_pairs={{4,0},{5,1},{6,2},{7,3},{8,4},{9,5},{10,6},{11,7},{12,8},{13,9},{1... | collective-permute-start | bytes 104456 | tf_op jit(solution)/shard_map/ppermute | solution.py:21
  395.3 12.2 %collective-permute-start.12 = (bf16[1,34,512]{2,1,0:T(8,128)(2,1)S(1)}, bf16[1,34,512]{2,1,0:T(8,128)(2,1)S(1)}, u32[]{:S(2)}, u32[]{:S(2)}) collective-permute-start(bf16[1,34,512]{2,1,0:T(8,128)(2,1)S(1)} %get-tuple-element.131), channel_id=1, source_target_pairs={{0,4},{1,5},{2,6},{3,7},{4,8},{5,9},{6,10},{7,11},{8,12},{9,13},{1... | collective-permute-start | bytes 104456 | tf_op jit(solution)/shard_map/ppermute | solution.py:21
  410.4 3.6 copy-start.2
  410.4 3.6 copy-start.4
  415.0 1.0 copy-start.3
  416.0 1.4 copy-start.8
Sparse Core Ops, SparseCore 0:
  10.4 134.9 all-gather.5
  148.6 118.1 all-gather.3
  270.0 106.7 all-gather.7
where the time goes:
time: 426 us; the launch traced here: 425 us
  waiting for transfers between devices  260 us (61%)
  starting transfers between devices  56.7 us (13%)
  local copies, waits for them, and re-layouts  43.5 us (10%)
  matrix products  31.6 us (7%)
  other arithmetic  19.1 us (4%)
  between operations  14.1 us (3%)
    all_gather x1, waiting for transfers between devices, on_device(): values_piece = lax.all_gather(values, 'seq', axis=0, tiled=True)  129 us
    all_gather x1, waiting for transfers between devices, on_device(): keys_piece = lax.all_gather(keys_ready, 'seq', axis=0, tiled=True)  113 us
    ppermute x14, starting transfers between devices, shifted(): return lax.ppermute(block, axis, route)  56.6 us
    broadcast_in_dim x28, local copies, waits for them, and re-layouts, on_device(): jnp.where(source_mask[:, None, None], arrived[None], jnp.zeros_like(slot_...  20.9 us
    ppermute x14, waiting for transfers between devices, shifted(): return lax.ppermute(block, axis, route)  17.8 us
    dot_general x2, matrix products, one_block(): jnp.einsum('qhd,khd->hqk', queries, keys_block, preferred_element_type=jn...  11 us
    dot_general x18, matrix products, conv_three(): jnp.dot(window, weight[tap_row, tap_col], preferred_element_type=jnp.floa...  9.62 us
    all_gather x1, local copies, waits for them, and re-layouts, on_device(): values_piece = lax.all_gather(values, 'seq', axis=0, tiled=True)  8.65 us
  transfers between devices with their start and end apart: 17, of which 6 were waited for; matrix products, arithmetic and copies ran while one was open for 20% of the time, Pallas kernels for 0%

commit v1 on v0

v1 whole, which is shorter than its diff:
```python
import math

import jax
import jax.numpy as jnp
import numpy as np
from jax import lax
from jax.experimental import pallas as pl
from jax.experimental.pallas import tpu as pltpu
from jax.sharding import PartitionSpec as P

GW = 64
THETA = 10000.0
EPS_NORM = 1e-06
LATENT_SCALE = 0.3611
LATENT_SHIFT = 0.1159
VMEM_LIMIT = 24 * 1024 * 1024
PREP_VMEM_LIMIT = 56 * 1024 * 1024

SLOTS = 16
PER_STEP = 3
STEP_SLOTS = 4
HALO_W = 18
HALO_H = 10
PIECE = 192
ROW_PITCH = 24
HEAD = 128
SHARE_SCALE = 16.0
GROUPS = 4
GROUP_START = (0, 5, 9, 13)
GROUP_ROWS = 80


def head_slot(head):
    return (head // PER_STEP) * STEP_SLOTS + head % PER_STEP


def rope_parts(grid_rows, grid_cols, head_dim):
    t_dims = head_dim // 8
    s_dims = (head_dim - t_dims) // 2
    pair = np.arange(head_dim) // 2
    t_pairs, s_pairs = t_dims // 2, s_dims // 2
    axis_id = np.where(pair < t_pairs, 0, np.where(pair < t_pairs + s_pairs, 1, 2))
    local = np.where(
        axis_id == 0, pair, np.where(axis_id == 1, pair - t_pairs, pair - t_pairs - s_pairs)
    )
    freq = (THETA ** (-2.0 * local / np.where(axis_id == 0, t_dims, s_dims))).astype(np.float32)
    row_angle = np.arange(grid_rows, dtype=np.float32)[:, None] * (freq * (axis_id == 1))
    col_angle = np.arange(grid_cols, dtype=np.float32)[:, None] * (freq * (axis_id == 2))
    tables = []
    for angle in (row_angle, col_angle):
        wide = angle.astype(np.float32).astype(np.float64)
        tables += [np.cos(wide).astype(np.float32), np.sin(wide).astype(np.float32)]
    return tables


def phase_selector(channels, i, j):
    shape = (256, 9 * channels)
    row = lax.broadcasted_iota(jnp.int32, shape, 0)
    col = lax.broadcasted_iota(jnp.int32, shape, 1)
    dr = 2 * (row >> 7) + ((row >> 1) & 1) + (i - 1)
    dc = 2 * ((row >> 6) & 1) + (row & 1) + (j - 1)
    target = (dr * 3 + dc) * channels + ((row & 63) >> 2)
    taken = (dr >= 0) & (dr < 3) & (dc >= 0) & (dc < 3) & (col == target)
    return jnp.where(taken, 1.0, 0.0).astype(jnp.bfloat16)


def prep_kernel(band_ref, q_ref, k_ref, v_ref, gain_ref, cr_ref, sr_ref, cc_ref, sc_ref, out_ref):
    tokens = q_ref.shape[0]
    band_rows = tokens // GW
    first = band_ref[0] * band_rows
    lane = lax.broadcasted_iota(jnp.int32, (GW, HEAD), 1)
    t_dims = HEAD // 8
    s_dims = (HEAD - t_dims) // 2
    on_cols = lane >= t_dims + s_dims
    cosine, sine = [], []
    for r in range(band_rows):
        cos_row = jnp.broadcast_to(cr_ref[pl.ds(first + r, 1), :], (GW, HEAD))
        sin_row = jnp.broadcast_to(sr_ref[pl.ds(first + r, 1), :], (GW, HEAD))
        cosine.append(jnp.where(on_cols, cc_ref[...], cos_row))
        sine.append(jnp.where(on_cols, sc_ref[...], sin_row))
    cosine = jnp.concatenate(cosine, axis=0)
    sine = jnp.concatenate(sine, axis=0)
    source = lax.broadcasted_iota(jnp.int32, (HEAD, HEAD), 0)
    target = lax.broadcasted_iota(jnp.int32, (HEAD, HEAD), 1)
    turn = jnp.where(
        (source ^ 1) == target, jnp.where((target & 1) == 0, -1.0, 1.0), 0.0
    ).astype(jnp.bfloat16)
    ones = jnp.full((HEAD, HEAD), 1.0, jnp.bfloat16)
    gains = gain_ref[...]
    even = lax.broadcasted_iota(jnp.int32, gains.shape, 1) % 2 == 0
    swapped = jnp.where(even, pltpu.roll(gains, HEAD - 1, 1), pltpu.roll(gains, 1, 1))

    def dot(x, y):
        return jnp.dot(x, y, preferred_element_type=jnp.float32)

    def ready(x, along, across):
        wide = x.astype(jnp.float32)
        squares = wide * wide
        high = squares.astype(jnp.bfloat16)
        low = (squares - high.astype(jnp.float32)).astype(jnp.bfloat16)
        mean = (dot(high, ones) + dot(low, ones)) * (1.0 / HEAD)
        turned = wide * along + dot(x, turn) * across
        return (turned * lax.rsqrt(mean + EPS_NORM)).astype(jnp.bfloat16)

    for which, ref in ((0, q_ref), (1, k_ref)):
        along = cosine * gains[which : which + 1, :]
        across = sine * swapped[which : which + 1, :]
        for h in range(PER_STEP):
            out_ref[h, which] = ready(ref[:, h * HEAD : (h + 1) * HEAD], along, across)
    for h in range(PER_STEP):
        out_ref[h, 2] = v_ref[:, h * HEAD : (h + 1) * HEAD]
    out_ref[PER_STEP] = jnp.zeros(out_ref.shape[1:], out_ref.dtype)


def prep(band, q, k, v, gain, tables):
    tokens = q.shape[0]
    wide = PER_STEP * HEAD
    rows = pl.BlockSpec((tokens, wide), lambda i, *_: (0, i))
    whole = lambda a: pl.BlockSpec(a.shape, lambda i, *_: (0, 0))
    return pl.pallas_call(
        prep_kernel,
        grid_spec=pltpu.PrefetchScalarGridSpec(
            num_scalar_prefetch=1,
            grid=(SLOTS // STEP_SLOTS,),
            in_specs=[rows, rows, rows, whole(gain)] + [whole(t) for t in tables],
            out_specs=pl.BlockSpec((STEP_SLOTS, 3, tokens, HEAD), lambda i, *_: (i, 0, 0, 0)),
        ),
        out_shape=jax.ShapeDtypeStruct((SLOTS, 3, tokens, HEAD), jnp.bfloat16),
        compiler_params=pltpu.CompilerParams(vmem_limit_bytes=PREP_VMEM_LIMIT),
        name="prep",
    )(band, q, k, v, gain, *tables)


def attend_kernel(place_ref, qkv_ref, wl_ref, out_ref, att_ref, cut_ref):
    sources, _, tok_dev, _ = qkv_ref.shape
    tokens = sources * tok_dev
    grid_rows = tokens // GW
    keys = qkv_ref[:, 1].reshape(tokens, HEAD)
    values = qkv_ref[:, 2].reshape(tokens, HEAD)
    factor = math.log2(math.e) / math.sqrt(HEAD)
    att_ref[0] = jnp.zeros(att_ref.shape[1:], jnp.float32)
    att_ref[grid_rows + 1] = jnp.zeros(att_ref.shape[1:], jnp.float32)
    edge = jnp.zeros((grid_rows + 2, 8, HEAD), jnp.float32)
    att_ref[:, 0:8, :] = edge
    att_ref[:, GW + 8 : GW + 16, :] = edge
    per_block = 2
    block = per_block * tok_dev
    block_rows = block // GW
    for b in range(sources // per_block):
        queries = qkv_ref[b * per_block : (b + 1) * per_block, 0].reshape(block, HEAD)
        scores = lax.dot_general(
            queries, keys, (((1,), (1,)), ((), ())), preferred_element_type=jnp.float32
        )
        highest = jnp.max(scores, axis=1, keepdims=True)
        weights = jnp.exp2((scores - highest) * factor)
        mass = jnp.sum(weights, axis=1, keepdims=True)
        summed = jnp.dot(weights.astype(jnp.bfloat16), values, preferred_element_type=jnp.float32)
        attended = (summed / mass).astype(jnp.bfloat16).astype(jnp.float32)
        att_ref[1 + b * block_rows : 1 + (b + 1) * block_rows, 8 : GW + 8, :] = attended.reshape(
            block_rows, GW, HEAD
        )
    side = math.isqrt(sources)
    for t in range(sources):
        top, left = (t // side) * (HALO_H - 2), (t % side) * (HALO_W - 2) + 7
        for r in range(HALO_H):
            cut_ref[t, r * HALO_W : (r + 1) * HALO_W, :] = att_ref[top + r, left : left + HALO_W, :]
        cut_ref[t, HALO_H * HALO_W : PIECE, :] = jnp.zeros(
            (PIECE - HALO_H * HALO_W, HEAD), jnp.float32
        )
    slot = place_ref[0]
    head = (slot // STEP_SLOTS) * PER_STEP + jnp.minimum(slot % STEP_SLOTS, PER_STEP - 1)
    weight = wl_ref[:, pl.ds(pl.multiple_of(head * HEAD, HEAD), HEAD)]
    empty = jnp.zeros_like(weight)
    weight = jnp.concatenate(
        [
            jnp.concatenate([weight, empty], axis=1),
            jnp.concatenate([empty, weight], axis=1),
        ],
        axis=0,
    )
    middle = PIECE // 2
    pairs = jnp.concatenate([cut_ref[:, :middle], cut_ref[:, middle:]], axis=2).astype(jnp.bfloat16)
    share = lax.dot_general(
        pairs.reshape(sources * middle, 2 * HEAD),
        weight,
        (((1,), (1,)), ((), ())),
        preferred_element_type=jnp.float32,
    )
    out_ref[...] = (share * SHARE_SCALE).reshape(out_ref.shape)


def attend(place, qkv, w_latent_t):
    sources, _, tok_dev, _ = qkv.shape
    tokens = sources * tok_dev
    return pl.pallas_call(
        attend_kernel,
        in_specs=[pl.BlockSpec(memory_space=pltpu.SMEM)] + [pl.BlockSpec(memory_space=pltpu.VMEM)] * 2,
        out_specs=pl.BlockSpec(memory_space=pltpu.VMEM),
        out_shape=jax.ShapeDtypeStruct((sources, PIECE // 2, 2 * w_latent_t.shape[0]), jnp.float32),
        scratch_shapes=[
            pltpu.VMEM((tokens // GW + 2, GW + 16, HEAD), jnp.float32),
            pltpu.VMEM((sources, PIECE, HEAD), jnp.float32),
        ],
        compiler_params=pltpu.CompilerParams(vmem_limit_bytes=VMEM_LIMIT),
        cost_estimate=pl.CostEstimate(
            flops=4 * tokens * tokens * HEAD,
            bytes_accessed=4 * tokens * HEAD * 2,
            transcendentals=tokens * tokens,
        ),
        name="attend",
    )(place, qkv, w_latent_t)


def tap_weight(ref, tap, channels):
    blocks = []
    for lane_block in range(2):
        halves = []
        for half in range(2):
            tile = 2 * tap + half
            group = max(g for g in range(GROUPS) if GROUP_START[g] <= tile)
            at = 16 * (tile - GROUP_START[group])
            halves.append(ref[lane_block * GROUPS + group, :, at : at + 16, :])
        blocks.append(jnp.concatenate(halves, axis=1).reshape(channels, 128))
    return jnp.concatenate(blocks, axis=1)


def hidden_kernel(
    heads, side, place_ref, part_ref, win_ref, bin_ref, x_ref, z_ref, flat_ref, hid_ref
):
    tile_row, tile_col = lax.div(place_ref[0], side), lax.rem(place_ref[0], side)
    grid_rows, grid_cols = side * (HALO_H - 2), side * (HALO_W - 2)
    top = tile_row * (HALO_H - 2) - 1
    left = tile_col * (HALO_W - 2) - 1

    latent = None
    for h in range(heads):
        share = part_ref[head_slot(h)]
        latent = share if latent is None else latent + share
    latent = (latent * (1.0 / SHARE_SCALE)).astype(jnp.bfloat16).astype(jnp.float32)
    z = (latent / LATENT_SCALE + LATENT_SHIFT).astype(jnp.bfloat16).astype(jnp.float32)
    crossed = pltpu.roll(z, 64, 1)
    first_half = lax.broadcasted_iota(jnp.int32, z.shape, 1) < 64
    z_ref[: PIECE // 2] = jnp.where(first_half, z, crossed)
    z_ref[PIECE // 2 :] = jnp.where(first_half, crossed, z)
    flat_ref[...] = jnp.zeros(flat_ref.shape, jnp.float32)
    col = left + lax.broadcasted_iota(jnp.int32, (HALO_W, 128), 0)
    for r in range(HALO_H):
        row = top + r
        inside = (col >= 0) & (col < grid_cols) & (row >= 0) & (row < grid_rows)
        start = ROW_PITCH * (r + 1) + 8
        flat_ref[start : start + HALO_W, :] = jnp.where(
            inside, z_ref[r * HALO_W : (r + 1) * HALO_W, :], 0.0
        )

    count = ROW_PITCH * HALO_H
    low = lax.broadcasted_iota(jnp.int32, (count, 128), 1) < 64
    out_col = left + lax.broadcasted_iota(jnp.int32, (ROW_PITCH, 128), 0)
    lane_blocks = hid_ref.shape[1]
    for i in range(2):
        for j in range(2):
            taps = []
            for a in (i - 1, i):
                at = 8 + ROW_PITCH * (1 + a) + (j - 1)
                taps.append(
                    jnp.where(low, flat_ref[at : at + count, :], flat_ref[at + 1 : at + 1 + count, :])
                )
            taps = jnp.concatenate(taps, axis=1).astype(jnp.bfloat16)
            weight = jnp.dot(
                phase_selector(win_ref.shape[0] // 9, i, j), win_ref[...], preferred_element_type=jnp.float32
            ).astype(jnp.bfloat16)
            pre = jnp.dot(taps, weight, preferred_element_type=jnp.float32) + bin_ref[...]
            hidden = (pre * (1.0 / (1.0 + jnp.exp(-pre)))).astype(jnp.bfloat16).astype(jnp.float32)
            for r in range(HALO_H):
                row = top + r
                inside = (out_col >= 0) & (out_col < grid_cols) & (row >= 0) & (row < grid_rows)
                for n in range(lane_blocks):
                    piece = hidden[r * ROW_PITCH : (r + 1) * ROW_PITCH, n * 128 : (n + 1) * 128]
                    hid_ref[2 * r + i, n, pl.ds(j, ROW_PITCH, stride=2), :] = jnp.where(
                        inside, piece, 0.0
                    )

    height, width = x_ref.shape[2] - 2, x_ref.shape[3]
    per_half = lane_blocks // 2
    for dc in range(3):
        for n in range(lane_blocks):
            x_ref[n // per_half, dc, :, :, (n % per_half) * 128 : (n % per_half + 1) * 128] = hid_ref[
                1 : height + 3, n, 1 + dc : 1 + dc + width, :
            ].astype(jnp.bfloat16)


def hidden_windows(place, part, w_in, b_in, heads, side):
    channels = w_in.shape[1]
    height, width = 2 * (HALO_H - 2), 2 * (HALO_W - 2)
    vmem = pl.BlockSpec(memory_space=pltpu.VMEM)
    return pl.pallas_call(
        lambda *refs: hidden_kernel(heads, side, *refs),
        in_specs=[pl.BlockSpec(memory_space=pltpu.SMEM)] + [vmem] * 3,
        out_specs=vmem,
        out_shape=jax.ShapeDtypeStruct((2, 3, height + 2, width, channels // 2), jnp.bfloat16),
        scratch_shapes=[
            pltpu.VMEM((PIECE, 128), jnp.float32),
            pltpu.VMEM((ROW_PITCH * (HALO_H + 2) + 16, 128), jnp.float32),
            pltpu.VMEM((2 * HALO_H, channels // 128, 2 * ROW_PITCH, 128), jnp.float32),
        ],
        compiler_params=pltpu.CompilerParams(vmem_limit_bytes=VMEM_LIMIT),
        cost_estimate=pl.CostEstimate(
            flops=8 * ROW_PITCH * HALO_H * 256 * channels,
            bytes_accessed=8 * height * width * channels,
            transcendentals=4 * ROW_PITCH * HALO_H * channels,
        ),
        name="hidden",
    )(place, part, w_in, b_in)


def decode_kernel(image_ref, x_ref, own_ref, other_ref, b_ref, out_ref):
    half = lax.rem(image_ref[0], 2)
    height, width = out_ref.shape[0], out_ref.shape[1]
    total = None
    depth = x_ref.shape[-1]
    channels = out_ref.shape[2]
    for dr in range(3):
        left_side, right_side = [], []
        for dc in range(3):
            for which, ref in ((half, own_ref), (1 - half, other_ref)):
                left_side.append(
                    x_ref[which, dc, dr : dr + height, :, :].reshape(height * width, depth)
                )
                right_side.append(tap_weight(ref, dr * 3 + dc, channels))
        part = lax.dot_general(
            jnp.concatenate(left_side, axis=1),
            jnp.concatenate(right_side, axis=1),
            (((1,), (1,)), ((), ())),
            preferred_element_type=jnp.float32,
        )
        total = part if total is None else total + part
    out_ref[...] = (total + b_ref[...]).astype(jnp.bfloat16).reshape(out_ref.shape)


def decode(image, windows, own, other, bias):
    channels = bias.shape[1]
    height, width = windows.shape[2] - 2, windows.shape[3]
    vmem = pl.BlockSpec(memory_space=pltpu.VMEM)
    return pl.pallas_call(
        decode_kernel,
        in_specs=[pl.BlockSpec(memory_space=pltpu.SMEM)] + [vmem] * 4,
        out_specs=vmem,
        out_shape=jax.ShapeDtypeStruct((height, width, channels), jnp.bfloat16),
        compiler_params=pltpu.CompilerParams(vmem_limit_bytes=VMEM_LIMIT),
        cost_estimate=pl.CostEstimate(
            flops=2 * height * width * 9 * channels * channels,
            bytes_accessed=2 * 9 * channels * channels,
            transcendentals=0,
        ),
        name="decode",
    )(image, windows, own, other, bias)


def on_device(
    query_rows, key_rows, value_rows, qk_gain, w_latent, conv_in_w, conv_in_b, conv_w, conv_b
):
    devices = lax.axis_size("seq")
    my_index = lax.axis_index("seq")
    my_image = lax.axis_index("img")
    tokens = devices * query_rows.shape[0]
    heads = query_rows.shape[1] // HEAD
    channels = conv_in_w.shape[3]
    own_channels = conv_w.shape[3]

    flipped = conv_w.reshape(9, channels, own_channels).transpose(0, 2, 1)
    flipped = flipped.reshape(9 * own_channels, channels)
    images = lax.axis_size("img")
    per_y = images // (2 * GROUPS)
    my_piece = my_image // per_y
    group = lax.rem(my_piece, GROUPS)
    start = 16 * (5 * group - jnp.maximum(group - 1, 0))
    lane = lax.rem(my_image, 2) * (channels // 2) + 128 * (my_piece // GROUPS)
    piece = lax.dynamic_slice(flipped, (start, lane), (GROUP_ROWS, 128))
    pieces = lax.all_to_all(
        jnp.broadcast_to(piece[None], (devices,) + piece.shape), "seq", 0, 0, tiled=True
    )

    tables = [jnp.asarray(t) for t in rope_parts(tokens // GW, GW, HEAD)]
    place = jnp.reshape(my_index, (1,)).astype(jnp.int32)
    image = jnp.reshape(my_image, (1,)).astype(jnp.int32)
    send = prep(place, query_rows, key_rows, value_rows, qk_gain, tables)
    qkv = lax.all_to_all(send, "seq", 0, 0, tiled=True)

    pieces, _ = lax.optimization_barrier((pieces, send))
    along_y = [[q + per_y * y for y in range(2 * GROUPS)] for q in range(per_y)]
    own = lax.all_gather(pieces, "img", axis=0, axis_index_groups=along_y)

    shares = attend(place, qkv, w_latent.T)
    part = lax.all_to_all(shares.astype(jnp.float16), "seq", 0, 0, tiled=True)
    part = part.astype(jnp.float32)

    windows = hidden_windows(
        place,
        part,
        conv_in_w.reshape(9 * conv_in_w.shape[2], channels),
        conv_in_b[None],
        heads,
        math.isqrt(devices),
    )
    own, _ = lax.optimization_barrier((own, shares))
    other = lax.ppermute(own, "img", [(i, i ^ 1) for i in range(images)])
    result = decode(image, windows, own, other, conv_b[None])
    return result[None]


def solution(mesh):
    placed = (
        P(("img", "seq"), None),
        P(("img", "seq"), None),
        P(("img", "seq"), None),
        P(),
        P(),
        P(),
        P(),
        P(None, None, None, "seq"),
        P(),
    )
    return jax.shard_map(
        on_device,
        mesh=mesh,
        in_specs=placed,
        out_specs=P(("img", "seq"), None, None, None),
        check_vma=False,
    )
```

time: 426 us -> 120 us (0.28)
  the two profiles are of different devices: /device:TPU:6 before, /device:TPU:40 now
where the time goes in v1:
time: 120 us; the launch traced here: 119 us
  blocking collectives  63.4 us (53%)
  Pallas kernels  16.3 us (14%)
  starting transfers between devices  15 us (12%)
  between operations  13.5 us (11%)
  waiting for transfers between devices  8.65 us (7%)
  local copies, waits for them, and re-layouts  2.24 us (2%)
    all_to_all x1, blocking collectives, on_device(): qkv = lax.all_to_all(send, 'seq', 0, 0, tiled=True)  43.4 us
    all_to_all x1, blocking collectives, on_device(): part = lax.all_to_all(shares.astype(jnp.float16), 'seq', 0, 0, tiled=True)  20 us
    all_to_all x1, starting transfers between devices, on_device(): lax.all_to_all(jnp.broadcast_to(piece[None], (devices,) + piece.shape), '...  12.9 us
    all_to_all x1, waiting for transfers between devices, on_device(): lax.all_to_all(jnp.broadcast_to(piece[None], (devices,) + piece.shape), '...  8.61 us
    pallas_call x1, Pallas kernels, attend(): pl.pallas_call(attend_kernel, in_specs=[pl.BlockSpec(memory_space=pltpu.S...  6.67 us
    pallas_call x1, Pallas kernels, prep(): pl.pallas_call(prep_kernel, grid_spec=pltpu.PrefetchScalarGridSpec(num_sc...  4.23 us
    pallas_call x1, Pallas kernels, decode(): pl.pallas_call(decode_kernel, in_specs=[pl.BlockSpec(memory_space=pltpu.S...  3.43 us
  transfers between devices with their start and end apart: 3, of which 1 were waited for; matrix products, arithmetic and copies ran while one was open for 0% of the time, Pallas kernels for 11%

profile of v1, /device:TPU:40, one launch (start us, length us, event | category | flops | bytes accessed | tf_op | source)
XLA Modules:
  0.0 119.1 jit_solution(5918197103914085232)
XLA Ops:
  6.5 0.7 dynamic_slice.3
  7.3 0.8 broadcast_in_dim.16
  8.0 12.9 %all-to-all-start.2 = ((bf16[16,80,128]{2,1,0:T(8,128)(2,1)}), bf16[16,80,128]{2,1,0:T(8,128)(2,1)S(1)}, u32[]{:S(2)}, u32[]{:S(2)}) async-start(bf16[16,80,128]{2,1,0:T(8,128)(2,1)} %broadcast_in_dim.16), calls=%async_computation.2 | async-start | bytes 655360 | tf_op jit(solution)/shard_map/all_to_all | solution.py:378
  20.9 0.0 all-gather.3.cloned.1.call-start
  21.0 4.2 %prep.1 = bf16[16,3,128,128]{3,2,1,0:T(8,128)(2,1)} custom-call(s32[1]{0:T(128)} %bitcast.1.band_ref.place_ref.refs_0_, bf16[128,1536]{1,0:T(8,128)(2,1)} %q_ref.1, bf16[128,1536]{1,0:T(8,128)(2,1)} %k_ref.1, bf16[128,1536]{1,0:T(8,128)(2,1)} %v_ref.1, f32[2,128]{1,0:T(2,128)} %gain_ref.1, f32[32,128]{1,0:T(8,128)} %constant.58.clone.cr_ref, ...), custom_call_target="tpu_custom_call" | custom-call | tf_op jit(solution)/shard_map/prep/pallas_call | solution.py:120
  25.2 0.0 copy-start.3
  25.2 8.6 %all-to-all-done.2 = bf16[16,80,128]{2,1,0:T(8,128)(2,1)S(1)} async-done(((bf16[16,80,128]{2,1,0:T(8,128)(2,1)}), bf16[16,80,128]{2,1,0:T(8,128)(2,1)S(1)}, u32[]{:S(2)}, u32[]{:S(2)}) %all-to-all-start.2) | async-done | bytes 327712 | tf_op jit(solution)/shard_map/all_to_all | solution.py:378
  33.8 0.0 copy-start.5
  33.8 0.7 copy-done.5
  34.5 0.0 all-gather.3.cloned.1.call-update
  34.6 43.4 %all_to_all.15.qkv_ref = bf16[16,3,128,128]{3,2,1,0:T(8,128)(2,1)S(1)} all-to-all(bf16[16,3,128,128]{3,2,1,0:T(8,128)(2,1)} %prep.1), channel_id=1, replica_groups=mesh['img'=32,'seq'=16] {'seq'}, dimensions={0} | all-to-all | bytes 3145728 | tf_op jit(solution)/shard_map/all_to_all | solution.py:386
  77.9 0.0 copy-done.3
  77.9 6.7 %attend.1 = f32[16,96,128]{2,1,0:T(8,128)S(1)} custom-call(s32[1]{0:T(128)} %bitcast.1.band_ref.place_ref.refs_0_, bf16[16,3,128,128]{3,2,1,0:T(8,128)(2,1)S(1)} %all_to_all.15.qkv_ref, bf16[64,1536]{1,0:T(8,128)(2,1)S(1)} %bitcast.17), custom_call_target="tpu_custom_call" | custom-call | flops 2147483648 | bytes 2097152 | tf_op jit(solution)/shard_map/attend/pallas_call | solution.py:195
  84.6 0.0 copy-start
  84.6 0.0 copy-start.1
  84.6 0.0 all-gather.3.cloned.1.call-done
  84.7 2.1 %collective-permute-start = (bf16[8,16,80,128]{3,2,1,0:T(8,128)(2,1)}, bf16[8,16,80,128]{3,2,1,0:T(8,128)(2,1)S(1)}, u32[]{:S(2)}, u32[]{:S(2)}) collective-permute-start(bf16[8,16,80,128]{3,2,1,0:T(8,128)(2,1)} %bitcast.15), channel_id=1, source_target_pairs={{0,16},{16,0},{32,48},{48,32},{64,80},{80,64},{96,112},{112,96},{1... | collective-permute-start | bytes 7864328 | tf_op jit(solution)/shard_map/ppermute | solution.py:405
  86.7 0.1 convert_element_type.6
  86.8 20.0 %all_to_all.16 = f16[16,96,128]{2,1,0:T(8,128)(2,1)S(1)} all-to-all(f16[16,96,128]{2,1,0:T(8,128)(2,1)S(1)} %convert_element_type.6), channel_id=1, replica_groups=mesh['img'=32,'seq'=16] {'seq'}, dimensions={0} | all-to-all | bytes 786432 | tf_op jit(solution)/shard_map/all_to_all | solution.py:393
  106.8 0.0 copy-start.2
  106.8 0.0 copy-start.4
  106.8 0.1 convert_element_type.7.refs_1_
  106.9 0.0 copy-done
  106.9 0.0 copy-done.1
  106.9 1.9 %hidden.1.x_ref = bf16[2,3,18,32,256]{4,3,2,1,0:T(8,128)(2,1)S(1)} custom-call(s32[1]{0:T(128)} %bitcast.1.band_ref.place_ref.refs_0_, f32[16,96,128]{2,1,0:T(8,128)S(1)} %convert_element_type.7.refs_1_, bf16[144,512]{1,0:T(8,128)(2,1)S(1)} %bitcast.13, f32[1,512]{1,0:T(1,128)S(1)} %bitcast.14), custom_call_target="tpu_custom_call" | custom-call | flops 251658240 | bytes 2097152 | tf_op jit(solution)/shard_map/hidden/pallas_call | solution.py:295
  108.8 0.0 collective-permute-done.other_ref
  108.8 0.0 copy-done.2
  108.8 0.0 copy-done.4
  108.9 3.4 %decode.1 = bf16[16,32,512]{2,1,0:T(8,128)(2,1)} custom-call(s32[1]{0:T(128)} %bitcast.image_ref, bf16[2,3,18,32,256]{4,3,2,1,0:T(8,128)(2,1)S(1)} %hidden.1.x_ref, bf16[8,16,80,128]{3,2,1,0:T(8,128)(2,1)S(1)} %bitcast.16, bf16[8,16,80,128]{3,2,1,0:T(8,128)(2,1)S(1)} %collective-permute-done.other_ref, f32[1,512]{1,0:T(1,128)S(1)} %bitcast.18), custom_call_target="tpu_custom_call" | custom-call | flops 2415919104 | bytes 4718592 | tf_op jit(solution)/shard_map/decode/pallas_call | solution.py:343
Async XLA Ops:
  8.0 25.8 %all-to-all-start.2 = ((bf16[16,80,128]{2,1,0:T(8,128)(2,1)}), bf16[16,80,128]{2,1,0:T(8,128)(2,1)S(1)}, u32[]{:S(2)}, u32[]{:S(2)}) async-start(bf16[16,80,128]{2,1,0:T(8,128)(2,1)} %broadcast_in_dim.16), calls=%async_computation.2 | async-start | bytes 655360 | tf_op jit(solution)/shard_map/all_to_all | solution.py:378
  20.9 63.7 %all-gather.3.cloned.1.call-start = ((), (), s32[]{:S(2)}) async-start(), calls=%async_computation.3 | async-start | bytes 2949120 | tf_op jit(solution)/shard_map/all_gather | solution.py:390
  25.2 52.7 %copy-start.3 = (bf16[1536,64]{0,1:T(8,128)(2,1)S(1)}, bf16[1536,64]{0,1:T(8,128)(2,1)}, u32[]{:S(2)}) copy-start(bf16[1536,64]{0,1:T(8,128)(2,1)} %param.17) | copy-start | bytes 589828
  33.8 0.7 copy-start.5
  84.6 22.3 %copy-start = (bf16[3,3,16,512]{3,2,1,0:T(8,128)(2,1)S(1)}, bf16[3,3,16,512]{3,2,1,0:T(8,128)(2,1)}, u32[]{:S(2)}) copy-start(bf16[3,3,16,512]{3,2,1,0:T(8,128)(2,1)} %param.18) | copy-start | bytes 442372
  84.6 22.3 %copy-start.1 = (f32[512]{0:T(512)S(1)}, f32[512]{0:T(512)}, u32[]{:S(2)}) copy-start(f32[512]{0:T(512)} %param.19) | copy-start | bytes 6148
  84.7 24.2 %collective-permute-start = (bf16[8,16,80,128]{3,2,1,0:T(8,128)(2,1)}, bf16[8,16,80,128]{3,2,1,0:T(8,128)(2,1)S(1)}, u32[]{:S(2)}, u32[]{:S(2)}) collective-permute-start(bf16[8,16,80,128]{3,2,1,0:T(8,128)(2,1)} %bitcast.15), channel_id=1, source_target_pairs={{0,16},{16,0},{32,48},{48,32},{64,80},{80,64},{96,112},{112,96},{1... | collective-permute-start | bytes 7864328 | tf_op jit(solution)/shard_map/ppermute | solution.py:405
  106.8 2.1 %copy-start.2 = (bf16[128,80,128]{2,1,0:T(8,128)(2,1)S(1)}, bf16[128,80,128]{2,1,0:T(8,128)(2,1)}, u32[]{:S(2)}) copy-start(bf16[128,80,128]{2,1,0:T(8,128)(2,1)} %all-gather.3.cloned.1.call-done) | copy-start | bytes 7864324
  106.8 2.1 %copy-start.4 = (f32[512]{0:T(512)S(1)}, f32[512]{0:T(512)}, u32[]{:S(2)}) copy-start(f32[512]{0:T(512)} %param.21) | copy-start | bytes 6148
Sparse Core Ops, SparseCore 0:
  34.7 38.9 all-gather.2

commit v2 on v1

--- a/solution.py
+++ b/solution.py
@@ -211,7 +211,7 @@
     )(place, qkv, w_latent_t)
 
 
-def tap_weight(ref, tap, channels):
+def tap_weight(ref, tap, channels, my_piece):
     blocks = []
     for lane_block in range(2):
         halves = []
@@ -219,7 +219,8 @@
             tile = 2 * tap + half
             group = max(g for g in range(GROUPS) if GROUP_START[g] <= tile)
             at = 16 * (tile - GROUP_START[group])
-            halves.append(ref[lane_block * GROUPS + group, :, at : at + 16, :])
+            shift = (my_piece + 2 * GROUPS - (lane_block * GROUPS + group)) & (2 * GROUPS - 1)
+            halves.append(ref[shift, :, at : at + 16, :])
         blocks.append(jnp.concatenate(halves, axis=1).reshape(channels, 128))
     return jnp.concatenate(blocks, axis=1)
 
@@ -312,8 +313,9 @@
     )(place, part, w_in, b_in)
 
 
-def decode_kernel(image_ref, x_ref, own_ref, other_ref, b_ref, out_ref):
+def decode_kernel(per_y, image_ref, x_ref, own_ref, other_ref, b_ref, out_ref):
     half = lax.rem(image_ref[0], 2)
+    my_piece = lax.div(image_ref[0], per_y)
     height, width = out_ref.shape[0], out_ref.shape[1]
     total = None
     depth = x_ref.shape[-1]
@@ -325,7 +327,7 @@
                 left_side.append(
                     x_ref[which, dc, dr : dr + height, :, :].reshape(height * width, depth)
                 )
-                right_side.append(tap_weight(ref, dr * 3 + dc, channels))
+                right_side.append(tap_weight(ref, dr * 3 + dc, channels, my_piece))
         part = lax.dot_general(
             jnp.concatenate(left_side, axis=1),
             jnp.concatenate(right_side, axis=1),
@@ -336,12 +338,12 @@
     out_ref[...] = (total + b_ref[...]).astype(jnp.bfloat16).reshape(out_ref.shape)
 
 
-def decode(image, windows, own, other, bias):
+def decode(image, windows, own, other, bias, per_y):
     channels = bias.shape[1]
     height, width = windows.shape[2] - 2, windows.shape[3]
     vmem = pl.BlockSpec(memory_space=pltpu.VMEM)
     return pl.pallas_call(
-        decode_kernel,
+        lambda *refs: decode_kernel(per_y, *refs),
         in_specs=[pl.BlockSpec(memory_space=pltpu.SMEM)] + [vmem] * 4,
         out_specs=vmem,
         out_shape=jax.ShapeDtypeStruct((height, width, channels), jnp.bfloat16),
@@ -383,13 +385,18 @@
     place = jnp.reshape(my_index, (1,)).astype(jnp.int32)
     image = jnp.reshape(my_image, (1,)).astype(jnp.int32)
     send = prep(place, query_rows, key_rows, value_rows, qk_gain, tables)
+    pieces, send = lax.optimization_barrier((pieces, send))
     qkv = lax.all_to_all(send, "seq", 0, 0, tiled=True)
 
-    pieces, _ = lax.optimization_barrier((pieces, send))
-    along_y = [[q + per_y * y for y in range(2 * GROUPS)] for q in range(per_y)]
-    own = lax.all_gather(pieces, "img", axis=0, axis_index_groups=along_y)
+    gathered = {0: pieces}
+    for k in (4, 3, 5, 2, 6, 1, 7):
+        route = [(i, (i + per_y * k) % images) for i in range(images)]
+        gathered[k] = lax.ppermute(pieces, "img", route)
 
     shares = attend(place, qkv, w_latent.T)
+    far = (4, 3, 5, 2, 6)
+    arrived, shares = lax.optimization_barrier(([gathered[k] for k in far], shares))
+    gathered.update(zip(far, arrived))
     part = lax.all_to_all(shares.astype(jnp.float16), "seq", 0, 0, tiled=True)
     part = part.astype(jnp.float32)
 
@@ -401,9 +408,10 @@
         heads,
         math.isqrt(devices),
     )
-    own, _ = lax.optimization_barrier((own, shares))
+    gathered, _ = lax.optimization_barrier((gathered, part))
+    own = jnp.stack([gathered[k] for k in range(2 * GROUPS)])
     other = lax.ppermute(own, "img", [(i, i ^ 1) for i in range(images)])
-    result = decode(image, windows, own, other, conv_b[None])
+    result = decode(image, windows, own, other, conv_b[None], per_y)
     return result[None]
 
 

time: 120 us -> 127 us (1.058)
  the two profiles are of different devices: /device:TPU:40 before, /device:TPU:6 now
where the time goes in v2:
time: 127 us; the launch traced here: 125 us
  starting transfers between devices  63.4 us (50%)
  waiting for transfers between devices  41.6 us (33%)
  Pallas kernels  16.3 us (13%)
  local copies, waits for them, and re-layouts  2.83 us (2%)
    ppermute x7, starting transfers between devices, on_device(): gathered[k] = lax.ppermute(pieces, 'img', route)  31.6 us
    ppermute x7, waiting for transfers between devices, on_device(): gathered[k] = lax.ppermute(pieces, 'img', route)  15.4 us
    all_to_all x1, starting transfers between devices, on_device(): lax.all_to_all(jnp.broadcast_to(piece[None], (devices,) + piece.shape), '...  13.3 us
    all_to_all x1, waiting for transfers between devices, on_device(): qkv = lax.all_to_all(send, 'seq', 0, 0, tiled=True)  12.2 us
    all_to_all x1, starting transfers between devices, on_device(): part = lax.all_to_all(shares.astype(jnp.float16), 'seq', 0, 0, tiled=True)  9.63 us
    all_to_all x1, starting transfers between devices, on_device(): qkv = lax.all_to_all(send, 'seq', 0, 0, tiled=True)  6.83 us
    pallas_call x1, Pallas kernels, attend(): pl.pallas_call(attend_kernel, in_specs=[pl.BlockSpec(memory_space=pltpu.S...  6.67 us
    all_to_all x1, waiting for transfers between devices, on_device(): lax.all_to_all(jnp.broadcast_to(piece[None], (devices,) + piece.shape), '...  6.44 us
  transfers between devices with their start and end apart: 11, of which 9 were waited for; matrix products, arithmetic and copies ran while one was open for 0% of the time, Pallas kernels for 10%

profile of v2, /device:TPU:6, one launch (start us, length us, event | category | flops | bytes accessed | tf_op | source)
XLA Modules:
  0.0 125.2 jit_solution(5150986542807558017)
XLA Ops:
  0.0 0.7 dynamic_slice.3
  0.7 0.8 broadcast_in_dim.15
  1.5 13.3 %all-to-all-start = ((bf16[16,80,128]{2,1,0:T(8,128)(2,1)}), bf16[16,80,128]{2,1,0:T(8,128)(2,1)S(1)}, u32[]{:S(2)}, u32[]{:S(2)}) async-start(bf16[16,80,128]{2,1,0:T(8,128)(2,1)} %broadcast_in_dim.15), calls=%async_computation | async-start | bytes 655360 | tf_op jit(solution)/shard_map/all_to_all | solution.py:380
  14.8 0.0 copy-start.2
  14.8 4.3 %prep.1 = bf16[16,3,128,128]{3,2,1,0:T(8,128)(2,1)} custom-call(s32[1]{0:T(128)} %bitcast.1.band_ref.place_ref.refs_0_, bf16[128,1536]{1,0:T(8,128)(2,1)} %q_ref.1, bf16[128,1536]{1,0:T(8,128)(2,1)} %k_ref.1, bf16[128,1536]{1,0:T(8,128)(2,1)} %v_ref.1, f32[2,128]{1,0:T(2,128)} %gain_ref.1, f32[32,128]{1,0:T(8,128)} %constant.58.clone.cr_ref, ...), custom_call_target="tpu_custom_call" | custom-call | tf_op jit(solution)/shard_map/prep/pallas_call | solution.py:120
  19.1 6.4 %all-to-all-done = bf16[16,80,128]{2,1,0:T(8,128)(2,1)S(1)} async-done(((bf16[16,80,128]{2,1,0:T(8,128)(2,1)}), bf16[16,80,128]{2,1,0:T(8,128)(2,1)S(1)}, u32[]{:S(2)}, u32[]{:S(2)}) %all-to-all-start) | async-done | bytes 327712 | tf_op jit(solution)/shard_map/all_to_all | solution.py:380
  25.5 6.8 %all-to-all-start.1 = ((bf16[16,3,128,128]{3,2,1,0:T(8,128)(2,1)}), bf16[16,3,128,128]{3,2,1,0:T(8,128)(2,1)S(1)}, u32[]{:S(2)}, u32[]{:S(2)}) async-start(bf16[16,3,128,128]{3,2,1,0:T(8,128)(2,1)} %prep.1), calls=%async_computation.1 | async-start | bytes 3145728 | tf_op jit(solution)/shard_map/all_to_all | solution.py:389
  32.3 7.7 %collective-permute-start = (bf16[16,80,128]{2,1,0:T(8,128)(2,1)S(1)}, bf16[16,80,128]{2,1,0:T(8,128)(2,1)S(1)}, u32[]{:S(2)}, u32[]{:S(2)}) collective-permute-start(bf16[16,80,128]{2,1,0:T(8,128)(2,1)S(1)} %all-to-all-done), channel_id=1, source_target_pairs={{0,256},{16,272},{32,288},{48,304},{64,320},{80,336},{96,352},{112... | collective-permute-start | bytes 983048 | tf_op jit(solution)/shard_map/ppermute | solution.py:394
  40.1 2.8 %collective-permute-start.1 = (bf16[16,80,128]{2,1,0:T(8,128)(2,1)S(1)}, bf16[16,80,128]{2,1,0:T(8,128)(2,1)S(1)}, u32[]{:S(2)}, u32[]{:S(2)}) collective-permute-start(bf16[16,80,128]{2,1,0:T(8,128)(2,1)S(1)} %all-to-all-done), channel_id=1, source_target_pairs={{0,192},{16,208},{32,224},{48,240},{64,256},{80,272},{96,288},{112... | collective-permute-start | bytes 983048 | tf_op jit(solution)/shard_map/ppermute | solution.py:394
  42.9 6.0 %collective-permute-start.2 = (bf16[16,80,128]{2,1,0:T(8,128)(2,1)S(1)}, bf16[16,80,128]{2,1,0:T(8,128)(2,1)S(1)}, u32[]{:S(2)}, u32[]{:S(2)}) collective-permute-start(bf16[16,80,128]{2,1,0:T(8,128)(2,1)S(1)} %all-to-all-done), channel_id=1, source_target_pairs={{0,320},{16,336},{32,352},{48,368},{64,384},{80,400},{96,416},{112... | collective-permute-start | bytes 983048 | tf_op jit(solution)/shard_map/ppermute | solution.py:394
  48.9 2.7 %collective-permute-start.3 = (bf16[16,80,128]{2,1,0:T(8,128)(2,1)S(1)}, bf16[16,80,128]{2,1,0:T(8,128)(2,1)}, u32[]{:S(2)}, u32[]{:S(2)}) collective-permute-start(bf16[16,80,128]{2,1,0:T(8,128)(2,1)S(1)} %all-to-all-done), channel_id=1, source_target_pairs={{0,128},{16,144},{32,160},{48,176},{64,192},{80,208},{96,224},{112... | collective-permute-start | bytes 983048 | tf_op jit(solution)/shard_map/ppermute | solution.py:394
  51.6 5.3 %collective-permute-start.4 = (bf16[16,80,128]{2,1,0:T(8,128)(2,1)S(1)}, bf16[16,80,128]{2,1,0:T(8,128)(2,1)S(1)}, u32[]{:S(2)}, u32[]{:S(2)}) collective-permute-start(bf16[16,80,128]{2,1,0:T(8,128)(2,1)S(1)} %all-to-all-done), channel_id=1, source_target_pairs={{0,384},{16,400},{32,416},{48,432},{64,448},{80,464},{96,480},{112... | collective-permute-start | bytes 983048 | tf_op jit(solution)/shard_map/ppermute | solution.py:394
  56.9 12.2 %all-to-all-done.1.qkv_ref = bf16[16,3,128,128]{3,2,1,0:T(8,128)(2,1)S(1)} async-done(((bf16[16,3,128,128]{3,2,1,0:T(8,128)(2,1)}), bf16[16,3,128,128]{3,2,1,0:T(8,128)(2,1)S(1)}, u32[]{:S(2)}, u32[]{:S(2)}) %all-to-all-start.1) | async-done | bytes 1572896 | tf_op jit(solution)/shard_map/all_to_all | solution.py:389
  69.1 0.0 copy-done.2
  69.1 6.7 %attend.1 = f32[16,96,128]{2,1,0:T(8,128)S(1)} custom-call(s32[1]{0:T(128)} %bitcast.1.band_ref.place_ref.refs_0_, bf16[16,3,128,128]{3,2,1,0:T(8,128)(2,1)S(1)} %all-to-all-done.1.qkv_ref, bf16[64,1536]{1,0:T(8,128)(2,1)S(1)} %bitcast.30), custom_call_target="tpu_custom_call" | custom-call | flops 2147483648 | bytes 2097152 | tf_op jit(solution)/shard_map/attend/pallas_call | solution.py:195
  75.8 0.0 collective-permute-done
  75.8 6.2 %collective-permute-done.1 = bf16[16,80,128]{2,1,0:T(8,128)(2,1)S(1)} collective-permute-done((bf16[16,80,128]{2,1,0:T(8,128)(2,1)S(1)}, bf16[16,80,128]{2,1,0:T(8,128)(2,1)S(1)}, u32[]{:S(2)}, u32[]{:S(2)}) %collective-permute-start.1) | collective-permute-done | bytes 327712 | tf_op jit(solution)/shard_map/ppermute | solution.py:394
  82.0 0.0 collective-permute-done.2
  82.0 6.3 %collective-permute-done.3 = bf16[16,80,128]{2,1,0:T(8,128)(2,1)} collective-permute-done((bf16[16,80,128]{2,1,0:T(8,128)(2,1)S(1)}, bf16[16,80,128]{2,1,0:T(8,128)(2,1)}, u32[]{:S(2)}, u32[]{:S(2)}) %collective-permute-start.3) | collective-permute-done | bytes 327712 | tf_op jit(solution)/shard_map/ppermute | solution.py:394
  88.3 1.3 %collective-permute-done.4 = bf16[16,80,128]{2,1,0:T(8,128)(2,1)S(1)} collective-permute-done((bf16[16,80,128]{2,1,0:T(8,128)(2,1)S(1)}, bf16[16,80,128]{2,1,0:T(8,128)(2,1)S(1)}, u32[]{:S(2)}, u32[]{:S(2)}) %collective-permute-start.4) | collective-permute-done | bytes 327712 | tf_op jit(solution)/shard_map/ppermute | solution.py:394
  89.6 0.8 convert_element_type.6
  90.4 9.6 %all-to-all-start.2 = ((f16[16,96,128]{2,1,0:T(8,128)(2,1)}), f16[16,96,128]{2,1,0:T(8,128)(2,1)S(1)}, u32[]{:S(2)}, u32[]{:S(2)}) async-start(f16[16,96,128]{2,1,0:T(8,128)(2,1)} %convert_element_type.6), calls=%async_computation.2 | async-start | bytes 786432 | tf_op jit(solution)/shard_map/all_to_all | solution.py:400
  100.1 2.9 %collective-permute-start.5 = (bf16[16,80,128]{2,1,0:T(8,128)(2,1)S(1)}, bf16[16,80,128]{2,1,0:T(8,128)(2,1)S(1)}, u32[]{:S(2)}, u32[]{:S(2)}) collective-permute-start(bf16[16,80,128]{2,1,0:T(8,128)(2,1)S(1)} %all-to-all-done), channel_id=1, source_target_pairs={{0,64},{16,80},{32,96},{48,112},{64,128},{80,144},{96,160},{112,17... | collective-permute-start | bytes 983048 | tf_op jit(solution)/shard_map/ppermute | solution.py:394
  103.0 4.1 %collective-permute-start.6 = (bf16[16,80,128]{2,1,0:T(8,128)(2,1)S(1)}, bf16[16,80,128]{2,1,0:T(8,128)(2,1)S(1)}, u32[]{:S(2)}, u32[]{:S(2)}) collective-permute-start(bf16[16,80,128]{2,1,0:T(8,128)(2,1)S(1)} %all-to-all-done), channel_id=1, source_target_pairs={{0,448},{16,464},{32,480},{48,496},{64,0},{80,16},{96,32},{112,48}... | collective-permute-start | bytes 983048 | tf_op jit(solution)/shard_map/ppermute | solution.py:394
  107.1 4.8 %all-to-all-done.2 = f16[16,96,128]{2,1,0:T(8,128)(2,1)S(1)} async-done(((f16[16,96,128]{2,1,0:T(8,128)(2,1)}), f16[16,96,128]{2,1,0:T(8,128)(2,1)S(1)}, u32[]{:S(2)}, u32[]{:S(2)}) %all-to-all-start.2) | async-done | bytes 393248 | tf_op jit(solution)/shard_map/all_to_all | solution.py:400
  111.9 0.1 convert_element_type.7.refs_1_
  112.0 0.0 copy-start
  112.0 0.0 copy-start.1
  112.0 0.1 collective-permute-done.5
  112.1 1.5 %collective-permute-done.6 = bf16[16,80,128]{2,1,0:T(8,128)(2,1)S(1)} collective-permute-done((bf16[16,80,128]{2,1,0:T(8,128)(2,1)S(1)}, bf16[16,80,128]{2,1,0:T(8,128)(2,1)S(1)}, u32[]{:S(2)}, u32[]{:S(2)}) %collective-permute-start.6) | collective-permute-done | bytes 327712 | tf_op jit(solution)/shard_map/ppermute | solution.py:394
  113.7 1.0 bitcast_dynamic-update-slice_fusion.5
  114.7 0.0 copy-start.3
  115.0 2.1 %collective-permute-start.7 = (bf16[8,16,80,128]{3,2,1,0:T(8,128)(2,1)S(1)}, bf16[8,16,80,128]{3,2,1,0:T(8,128)(2,1)S(1)}, u32[]{:S(2)}, u32[]{:S(2)}) collective-permute-start(bf16[8,16,80,128]{3,2,1,0:T(8,128)(2,1)S(1)} %bitcast_dynamic-update-slice_fusion.refs_2_), channel_id=1, source_target_pairs={{0,16},{16,0},{32,48},{48,32},{64,80},{80,64},{96,112},{112,96},{1... | collective-permute-start | bytes 7864328 | tf_op jit(solution)/shard_map/ppermute | solution.py:413
  117.1 0.0 copy-done
  117.1 0.0 copy-done.1
  117.1 1.9 %hidden.1.refs_1_ = bf16[2,3,18,32,256]{4,3,2,1,0:T(8,128)(2,1)S(1)} custom-call(s32[1]{0:T(128)} %bitcast.1.band_ref.place_ref.refs_0_, f32[16,96,128]{2,1,0:T(8,128)S(1)} %convert_element_type.7.refs_1_, bf16[144,512]{1,0:T(8,128)(2,1)S(1)} %bitcast.28, f32[1,512]{1,0:T(1,128)S(1)} %bitcast.29), custom_call_target="tpu_custom_call" | custom-call | flops 251658240 | bytes 2097152 | tf_op jit(solution)/shard_map/hidden/pallas_call | solution.py:296
  119.0 2.8 %collective-permute-done.7.refs_3_ = bf16[8,16,80,128]{3,2,1,0:T(8,128)(2,1)S(1)} collective-permute-done((bf16[8,16,80,128]{3,2,1,0:T(8,128)(2,1)S(1)}, bf16[8,16,80,128]{3,2,1,0:T(8,128)(2,1)S(1)}, u32[]{:S(2)}, u32[]{:S(2)}) %collective-permute-start.7) | collective-permute-done | bytes 2621472 | tf_op jit(solution)/shard_map/ppermute | solution.py:413
  121.8 0.0 copy-done.3
  121.8 3.4 %decode.1 = bf16[16,32,512]{2,1,0:T(8,128)(2,1)} custom-call(s32[1]{0:T(128)} %bitcast.refs_0_, bf16[2,3,18,32,256]{4,3,2,1,0:T(8,128)(2,1)S(1)} %hidden.1.refs_1_, bf16[8,16,80,128]{3,2,1,0:T(8,128)(2,1)S(1)} %bitcast_dynamic-update-slice_fusion.refs_2_, bf16[8,16,80,128]{3,2,1,0:T(8,128)(2,1)S(1)} %collective-permute-done.7.refs_3_, f32[1,512]{1,0:T(1,128)S(1)} %bitcast.31), custom_call_target="tpu_custom_call" | custom-call | flops 2415919104 | bytes 4718592 | tf_op jit(solution)/shard_map/decode/pallas_call | solution.py:345
  (7 shorter events, 0.3 us)
Async XLA Ops:
  1.5 24.0 %all-to-all-start = ((bf16[16,80,128]{2,1,0:T(8,128)(2,1)}), bf16[16,80,128]{2,1,0:T(8,128)(2,1)S(1)}, u32[]{:S(2)}, u32[]{:S(2)}) async-start(bf16[16,80,128]{2,1,0:T(8,128)(2,1)} %broadcast_in_dim.15), calls=%async_computation | async-start | bytes 655360 | tf_op jit(solution)/shard_map/all_to_all | solution.py:380
  14.8 54.3 %copy-start.2 = (bf16[1536,64]{0,1:T(8,128)(2,1)S(1)}, bf16[1536,64]{0,1:T(8,128)(2,1)}, u32[]{:S(2)}) copy-start(bf16[1536,64]{0,1:T(8,128)(2,1)} %param.17) | copy-start | bytes 589828
  25.5 43.6 %all-to-all-start.1 = ((bf16[16,3,128,128]{3,2,1,0:T(8,128)(2,1)}), bf16[16,3,128,128]{3,2,1,0:T(8,128)(2,1)S(1)}, u32[]{:S(2)}, u32[]{:S(2)}) async-start(bf16[16,3,128,128]{3,2,1,0:T(8,128)(2,1)} %prep.1), calls=%async_computation.1 | async-start | bytes 3145728 | tf_op jit(solution)/shard_map/all_to_all | solution.py:389
  32.3 43.4 %collective-permute-start = (bf16[16,80,128]{2,1,0:T(8,128)(2,1)S(1)}, bf16[16,80,128]{2,1,0:T(8,128)(2,1)S(1)}, u32[]{:S(2)}, u32[]{:S(2)}) collective-permute-start(bf16[16,80,128]{2,1,0:T(8,128)(2,1)S(1)} %all-to-all-done), channel_id=1, source_target_pairs={{0,256},{16,272},{32,288},{48,304},{64,320},{80,336},{96,352},{112... | collective-permute-start | bytes 983048 | tf_op jit(solution)/shard_map/ppermute | solution.py:394
  40.1 41.9 %collective-permute-start.1 = (bf16[16,80,128]{2,1,0:T(8,128)(2,1)S(1)}, bf16[16,80,128]{2,1,0:T(8,128)(2,1)S(1)}, u32[]{:S(2)}, u32[]{:S(2)}) collective-permute-start(bf16[16,80,128]{2,1,0:T(8,128)(2,1)S(1)} %all-to-all-done), channel_id=1, source_target_pairs={{0,192},{16,208},{32,224},{48,240},{64,256},{80,272},{96,288},{112... | collective-permute-start | bytes 983048 | tf_op jit(solution)/shard_map/ppermute | solution.py:394
  42.9 39.1 %collective-permute-start.2 = (bf16[16,80,128]{2,1,0:T(8,128)(2,1)S(1)}, bf16[16,80,128]{2,1,0:T(8,128)(2,1)S(1)}, u32[]{:S(2)}, u32[]{:S(2)}) collective-permute-start(bf16[16,80,128]{2,1,0:T(8,128)(2,1)S(1)} %all-to-all-done), channel_id=1, source_target_pairs={{0,320},{16,336},{32,352},{48,368},{64,384},{80,400},{96,416},{112... | collective-permute-start | bytes 983048 | tf_op jit(solution)/shard_map/ppermute | solution.py:394
  48.9 39.4 %collective-permute-start.3 = (bf16[16,80,128]{2,1,0:T(8,128)(2,1)S(1)}, bf16[16,80,128]{2,1,0:T(8,128)(2,1)}, u32[]{:S(2)}, u32[]{:S(2)}) collective-permute-start(bf16[16,80,128]{2,1,0:T(8,128)(2,1)S(1)} %all-to-all-done), channel_id=1, source_target_pairs={{0,128},{16,144},{32,160},{48,176},{64,192},{80,208},{96,224},{112... | collective-permute-start | bytes 983048 | tf_op jit(solution)/shard_map/ppermute | solution.py:394
  51.6 38.0 %collective-permute-start.4 = (bf16[16,80,128]{2,1,0:T(8,128)(2,1)S(1)}, bf16[16,80,128]{2,1,0:T(8,128)(2,1)S(1)}, u32[]{:S(2)}, u32[]{:S(2)}) collective-permute-start(bf16[16,80,128]{2,1,0:T(8,128)(2,1)S(1)} %all-to-all-done), channel_id=1, source_target_pairs={{0,384},{16,400},{32,416},{48,432},{64,448},{80,464},{96,480},{112... | collective-permute-start | bytes 983048 | tf_op jit(solution)/shard_map/ppermute | solution.py:394
  90.4 21.5 %all-to-all-start.2 = ((f16[16,96,128]{2,1,0:T(8,128)(2,1)}), f16[16,96,128]{2,1,0:T(8,128)(2,1)S(1)}, u32[]{:S(2)}, u32[]{:S(2)}) async-start(f16[16,96,128]{2,1,0:T(8,128)(2,1)} %convert_element_type.6), calls=%async_computation.2 | async-start | bytes 786432 | tf_op jit(solution)/shard_map/all_to_all | solution.py:400
  100.1 12.1 %collective-permute-start.5 = (bf16[16,80,128]{2,1,0:T(8,128)(2,1)S(1)}, bf16[16,80,128]{2,1,0:T(8,128)(2,1)S(1)}, u32[]{:S(2)}, u32[]{:S(2)}) collective-permute-start(bf16[16,80,128]{2,1,0:T(8,128)(2,1)S(1)} %all-to-all-done), channel_id=1, source_target_pairs={{0,64},{16,80},{32,96},{48,112},{64,128},{80,144},{96,160},{112,17... | collective-permute-start | bytes 983048 | tf_op jit(solution)/shard_map/ppermute | solution.py:394
  103.0 10.6 %collective-permute-start.6 = (bf16[16,80,128]{2,1,0:T(8,128)(2,1)S(1)}, bf16[16,80,128]{2,1,0:T(8,128)(2,1)S(1)}, u32[]{:S(2)}, u32[]{:S(2)}) collective-permute-start(bf16[16,80,128]{2,1,0:T(8,128)(2,1)S(1)} %all-to-all-done), channel_id=1, source_target_pairs={{0,448},{16,464},{32,480},{48,496},{64,0},{80,16},{96,32},{112,48}... | collective-permute-start | bytes 983048 | tf_op jit(solution)/shard_map/ppermute | solution.py:394
  112.0 5.1 %copy-start = (bf16[3,3,16,512]{3,2,1,0:T(8,128)(2,1)S(1)}, bf16[3,3,16,512]{3,2,1,0:T(8,128)(2,1)}, u32[]{:S(2)}) copy-start(bf16[3,3,16,512]{3,2,1,0:T(8,128)(2,1)} %param.18) | copy-start | bytes 442372
  112.0 5.1 %copy-start.1 = (f32[512]{0:T(512)S(1)}, f32[512]{0:T(512)}, u32[]{:S(2)}) copy-start(f32[512]{0:T(512)} %param.19) | copy-start | bytes 6148
  114.7 7.0 %copy-start.3 = (f32[512]{0:T(512)S(1)}, f32[512]{0:T(512)}, u32[]{:S(2)}) copy-start(f32[512]{0:T(512)} %param.21) | copy-start | bytes 6148
  115.0 6.8 %collective-permute-start.7 = (bf16[8,16,80,128]{3,2,1,0:T(8,128)(2,1)S(1)}, bf16[8,16,80,128]{3,2,1,0:T(8,128)(2,1)S(1)}, u32[]{:S(2)}, u32[]{:S(2)}) collective-permute-start(bf16[8,16,80,128]{3,2,1,0:T(8,128)(2,1)S(1)} %bitcast_dynamic-update-slice_fusion.refs_2_), channel_id=1, source_target_pairs={{0,16},{16,0},{32,48},{48,32},{64,80},{80,64},{96,112},{112,96},{1... | collective-permute-start | bytes 7864328 | tf_op jit(solution)/shard_map/ppermute | solution.py:413
